TPU v7x, 32 devices: a whole 2x2x4 slice. The times are simulated.
32 devices in a mesh: probe: 2 (over x), row: 4 (over y, core), col: 4 (over z).
Axes of the slice: x: 2, y: 2, z: 4, core: 2. Of those that a mesh axis runs over, the one named last changes fastest.
Arguments:
- flow_state: bfloat16 [2, 5, 192, 192, 384], P('probe', None, 'row', 'col'), may hold values from -6 to 6
- forcing: bfloat16 [2, 5, 192, 192, 384], P('probe', None, 'row', 'col'), may hold values from -6 to 6
- advect_x: bfloat16 [192, 192, 384], P('row', 'col'), may hold values from 0.19921875 to 1.5
- advect_y: bfloat16 [192, 192, 384], P('row', 'col'), may hold values from 0.19921875 to 1.5
- advect_z: bfloat16 [192, 192, 384], P('row', 'col'), may hold values from 0.19921875 to 1.5
- diffusivity: float32 [5], replicated, may hold values from 0.2 to 1
- deriv_x: bfloat16 [2, 384, 384], replicated, may hold values from -0.3125 to 0.3125
- deriv_y: bfloat16 [2, 192, 192], replicated, may hold values from -0.4375 to 0.4375
- deriv_z: bfloat16 [2, 192, 192], replicated, may hold values from -0.4375 to 0.4375
- test_mix: float32 [2, 2], replicated, may hold values from -4 to 4
Outputs:
- section_out: bfloat16 [2, 5, 192, 192, 384], P('probe', None, 'row', 'col')
- sketch: bfloat16 [2, 5, 192, 192, 384], P(None, None, 'row', 'col', 'probe')
All inputs are finite; a program needn't handle non-finite values.
Results may differ from a plain program's by a relative error of at most 0.0095.
Values may be sent and summed in bfloat16 or wider, within the bound.
A program may use at most 256 MiB of HBM per device.

v0:
```python
import jax
import jax.numpy as jnp
from jax import lax
from jax.sharding import PartitionSpec as P

step_size = 0.25


def on_device(
    flow_state,
    forcing,
    advect_x,
    advect_y,
    advect_z,
    diffusivity,
    deriv_x,
    deriv_y,
    deriv_z,
    test_mix,
):
    frc_dev, nvars, ny_loc, nz_loc, nx_all = flow_state.shape
    flat_count = frc_dev * nvars
    coeff = diffusivity.reshape(1, -1, 1, 1, 1)
    coeff_flat = jnp.tile(diffusivity, frc_dev).reshape(flat_count, 1, 1, 1)
    grad_x = jnp.einsum(
        "fvyzj,kij->kfvyzi", flow_state, deriv_x, preferred_element_type=jnp.float32
    )
    term_x = -advect_x[None, None] * grad_x[0] + coeff * grad_x[1]
    flat_state = flow_state.reshape(flat_count, ny_loc, nz_loc, nx_all)
    stack_y = jnp.concatenate([flat_state, advect_y[None]], axis=0)
    recv_y = lax.all_to_all(stack_y, "row", split_axis=3, concat_axis=1, tiled=True)
    grads_y = jnp.einsum(
        "cjzx,kij->kcizx", recv_y[:flat_count], deriv_y, preferred_element_type=jnp.float32
    )
    term_y = (-recv_y[flat_count][None] * grads_y[0] + coeff_flat * grads_y[1]).astype(jnp.bfloat16)
    back_y = lax.all_to_all(term_y, "row", split_axis=1, concat_axis=3, tiled=True)
    stack_z = jnp.concatenate([flat_state, advect_z[None]], axis=0)
    recv_z = lax.all_to_all(stack_z, "col", split_axis=3, concat_axis=2, tiled=True)
    grads_z = jnp.einsum(
        "cyjx,kij->kcyix", recv_z[:flat_count], deriv_z, preferred_element_type=jnp.float32
    )
    term_z = (-recv_z[flat_count][None] * grads_z[0] + coeff_flat * grads_z[1]).astype(jnp.bfloat16)
    back_z = lax.all_to_all(term_z, "col", split_axis=2, concat_axis=3, tiled=True)
    back_y = back_y.reshape(flow_state.shape)
    back_z = back_z.reshape(flow_state.shape)
    total_rhs = (
        term_x
        + back_y.astype(jnp.float32)
        + back_z.astype(jnp.float32)
        + forcing.astype(jnp.float32)
    )
    section_out = (flow_state.astype(jnp.float32) + step_size * total_rhs).astype(jnp.bfloat16)
    mix_rows = lax.dynamic_slice_in_dim(test_mix, lax.axis_index("probe") * frc_dev, frc_dev, 0)
    partial_value = (
        section_out[0].astype(jnp.float32)[None] * mix_rows[0][:, None, None, None, None]
    )
    partial_value = lax.optimization_barrier(partial_value.astype(jnp.bfloat16)).astype(jnp.float32)
    sketch = lax.psum_scatter(
        partial_value.astype(jnp.bfloat16), "probe", scatter_dimension=4, tiled=True
    )
    return (section_out, sketch)


def solution(mesh):
    placed = (
        P("probe", None, "row", "col", None),
        P("probe", None, "row", "col", None),
        P("row", "col", None),
        P("row", "col", None),
        P("row", "col", None),
        P(),
        P(),
        P(),
        P(),
        P(),
    )
    return jax.shard_map(
        on_device,
        mesh=mesh,
        in_specs=placed,
        out_specs=(P("probe", None, "row", "col", None), P(None, None, "row", "col", "probe")),
        check_vma=False,
    )
```

profile of v0, /device:TPU:0, one launch (start us, length us, event | category | flops | bytes accessed | tf_op | source)
XLA Modules:
  0.0 1445.8 jit_solution(16954068725476881595)
XLA Ops:
  20.2 37.9 %copy.69 = bf16[6,48,48,384]{2,1,0,3:T(8,128)(2,1)} copy(bf16[6,48,48,384]{3,2,1,0:T(8,128)(2,1)} %get-tuple-element.4) | data formatting | bytes 21233664 | tf_op jit(solution)/shard_map/concatenate | solution.py:30
  58.0 60.2 %reshape.138 = bf16[4,2,663552]{2,1,0:T(2,128)(2,1)} reshape(bf16[384,6,48,48]{3,2,1,0:T(8,128)(2,1)} %bitcast.127) | data formatting | bytes 21233664
  124.3 37.9 %copy.79 = bf16[6,48,48,384]{2,1,0,3:T(8,128)(2,1)} copy(bf16[6,48,48,384]{3,2,1,0:T(8,128)(2,1)} %get-tuple-element.5) | data formatting | bytes 21233664 | tf_op jit(solution)/shard_map/concatenate | solution.py:37
  162.2 60.4 %reshape.136 = bf16[4,2,663552]{2,1,0:T(2,128)(2,1)} reshape(bf16[384,6,48,48]{3,2,1,0:T(8,128)(2,1)} %bitcast.128) | data formatting | bytes 21233664
  222.6 19.4 %all-to-all-done = bf16[4,2,663552]{2,1,0:T(2,128)(2,1)} async-done(((bf16[4,2,663552]{2,1,0:T(2,128)(2,1)}), bf16[4,2,663552]{2,1,0:T(2,128)(2,1)}, u32[]{:S(2)}, u32[]{:S(2)}) %all-to-all-start) | async-done | bytes 10616864 | tf_op jit(solution)/shard_map/all_to_all | solution.py:31
  259.0 44.8 %reshape.139 = bf16[384,6,48,48]{3,2,1,0:T(8,128)(2,1)} reshape(bf16[4,2,663552]{2,1,0:T(2,128)(2,1)} %all-to-all-done) | data formatting | bytes 21233664
  303.8 36.1 %copy.94 = bf16[6,48,48,4,96]{4,3,2,1,0:T(4,128)(2,1)} copy(bf16[6,48,48,4,96]{2,1,0,4,3:T(8,128)(2,1)} %bitcast.129) | data formatting | bytes 21233664 | tf_op jit(solution)/shard_map/all_to_all | solution.py:31
  365.6 25.7 %convolution_bitcast_fusion.1 = f32[2,5,192,48,96]{2,4,0,3,1:T(8,128)} fusion(bf16[5,192,48,96,1]{3,2,1,0,4:T(8,128)(2,1)} %bitcast.137, bf16[2,192,192]{2,1,0:T(8,128)(2,1)S(1)} %copy-done.4), kind=kOutput, calls=%fused_computation.27 | convolution fusion | flops 3397386240 | bytes 44384256 | tf_op jit(solution)/shard_map/cjzx,kij->kcizx/dot_general | solution.py:32
  391.3 19.9 %fusion.6 = bf16[5,192,48,96]{1,3,2,0:T(8,128)(2,1)} fusion(f32[2,5,192,48,96]{2,4,0,3,1:T(8,128)} %convolution_bitcast_fusion.1, f32[5]{0:T(128)S(1)} %copy-done.6, f32[192,48,96]{0,2,1:T(8,128)S(1)} %copy-done.2), kind=kLoop, calls=%fused_computation.10 | loop fusion | flops 17694720 | bytes 47775764 | tf_op jit(solution)/shard_map/convert_element_type | solution.py:35
  428.5 62.1 %all-to-all-done.2 = bf16[4,2,663552]{2,1,0:T(2,128)(2,1)} async-done(((bf16[4,2,663552]{2,1,0:T(2,128)(2,1)}), bf16[4,2,663552]{2,1,0:T(2,128)(2,1)}, u32[]{:S(2)}, u32[]{:S(2)}) %all-to-all-start.2) | async-done | bytes 10616864 | tf_op jit(solution)/shard_map/all_to_all | solution.py:38
  497.0 44.8 %reshape.137 = bf16[384,6,48,48]{3,2,1,0:T(8,128)(2,1)} reshape(bf16[4,2,663552]{2,1,0:T(2,128)(2,1)} %all-to-all-done.2) | data formatting | bytes 21233664
  541.8 36.1 %copy.97 = bf16[6,48,48,4,96]{4,3,2,1,0:T(4,128)(2,1)} copy(bf16[6,48,48,4,96]{2,1,0,4,3:T(8,128)(2,1)} %bitcast.130) | data formatting | bytes 21233664 | tf_op jit(solution)/shard_map/all_to_all | solution.py:38
  602.8 23.6 %convolution_bitcast_fusion = f32[2,5,48,192,96]{3,4,0,2,1:T(8,128)} fusion(bf16[5,48,192,96,1]{3,2,4,1,0:T(8,128)(2,1)} %bitcast.138, bf16[2,192,192]{2,1,0:T(8,128)(2,1)S(1)} %copy-done.5), kind=kOutput, calls=%fused_computation.26 | convolution fusion | flops 3397386240 | bytes 44384256 | tf_op jit(solution)/shard_map/cyjx,kij->kcyix/dot_general | solution.py:39
  626.4 21.7 %fusion.2 = bf16[5,48,192,96]{2,3,1,0:T(8,128)(2,1)} fusion(f32[2,5,48,192,96]{3,4,0,2,1:T(8,128)} %convolution_bitcast_fusion, f32[5]{0:T(128)S(1)} %copy-done.6, f32[48,192,96]{1,2,0:T(8,128)} %copy.82), kind=kLoop, calls=%fused_computation.4 | loop fusion | flops 17694720 | bytes 47775764 | tf_op jit(solution)/shard_map/convert_element_type | solution.py:42
  673.9 18.6 %fusion.18 = f32[2,384,5,48,48]{1,4,3,2,0:T(8,128)} fusion(bf16[1,5,48,48,384]{4,3,2,1,0:T(8,128)(2,1)} %param.10, bf16[2,384,384]{2,1,0:T(8,128)(2,1)S(1)} %copy-done), kind=kOutput, calls=%fused_computation.32 | convolution fusion | flops 6794772480 | bytes 44826624 | tf_op jit(solution)/shard_map/fvyzj,kij->kfvyzi/dot_general | solution.py:25
  717.4 24.5 %reshape.122 = f32[1,5,48,48,384]{4,3,2,1,0:T(8,128)} reshape(f32[5,48,48,4,96]{4,3,2,1,0:T(4,128)} %copy.78) | data formatting | bytes 35389440 | tf_op jit(solution)/shard_map/convert_element_type | solution.py:48
  741.9 186.9 %all-to-all-done.3 = bf16[5,48,192,96]{3,1,0,2:T(8,128)(2,1)} async-done(((bf16[5,48,192,96]{3,1,0,2:T(8,128)(2,1)}), bf16[5,48,192,96]{3,1,0,2:T(8,128)(2,1)}, u32[]{:S(2)}, u32[]{:S(2)}) %all-to-all-start.3) | async-done | bytes 8847392 | tf_op jit(solution)/shard_map/all_to_all | solution.py:43
  948.8 24.5 %reshape.124 = f32[1,5,48,48,384]{4,3,2,1,0:T(8,128)} reshape(f32[5,48,48,4,96]{4,3,2,1,0:T(4,128)} %copy.88) | data formatting | bytes 35389440 | tf_op jit(solution)/shard_map/convert_element_type | solution.py:49
  973.3 38.7 %bitcast_convert_fusion = (f32[5,48,48,384]{3,2,1,0:T(8,128)}, bf16[1,5,48,48,384]{4,3,2,1,0:T(8,128)(2,1)}) fusion(bf16[1,5,48,48,384]{4,3,2,1,0:T(8,128)(2,1)} %param.11, f32[1,5,48,48,384]{4,3,2,1,0:T(8,128)} %reshape.124, f32[1,5,48,48,384]{4,3,2,1,0:T(8,128)} %reshape.122, f32[2,1,5,48,48,384]{5,4,3,2,0,1:T(8,128)} %bitcast.124, f32[5]{0:T(128)S(1)} %copy-done.6, ...), kind=kLoop, calls=%fused_computation.31 | loop fusion | flops 53084160 | bytes 118554640 | tf_op jit(solution)/shard_map/mul | solution.py:55
  1029.5 61.8 %copy.100 = bf16[2,5,48,48,384]{3,2,1,0,4:T(8,128)(2,1)} copy(bf16[2,5,48,48,384]{4,3,2,1,0:T(8,128)(2,1)} %multiply_convert_fusion) | data formatting | bytes 35389440
  1091.3 89.9 %reshape.134 = bf16[384,23040]{1,0:T(8,128)(2,1)} reshape(bf16[384,2,5,48,48]{4,3,2,1,0:T(8,128)(2,1)} %bitcast.126) | data formatting | bytes 35389440
  1181.2 198.4 %reduce-scatter.4.cloned.1.call-done = bf16[192,23040]{1,0:T(8,128)(2,1)} async-done(((bf16[384,23040]{1,0:T(8,128)(2,1)}), bf16[192,23040]{1,0:T(8,128)(2,1)}) %reduce-scatter.4.cloned.1.call-update) | async-done | bytes 8847376
  1379.6 28.4 %reshape.135 = bf16[192,2,5,48,48]{4,3,2,1,0:T(8,128)(2,1)} reshape(bf16[192,23040]{1,0:T(8,128)(2,1)} %reduce-scatter.4.cloned.1.call-done) | data formatting | bytes 17694720
  1408.0 30.7 %copy.101 = bf16[2,5,48,48,192]{4,3,2,1,0:T(8,128)(2,1)} copy(bf16[2,5,48,48,192]{3,2,1,0,4:T(8,128)(2,1)} %bitcast.132) | data formatting | bytes 17694720
  (45 shorter events, 198.6 us)
Async XLA Ops:
  7.2 666.7 %copy-start = (bf16[2,384,384]{2,1,0:T(8,128)(2,1)S(1)}, bf16[2,384,384]{2,1,0:T(8,128)(2,1)}, u32[]{:S(2)}) copy-start(bf16[2,384,384]{2,1,0:T(8,128)(2,1)} %param.16) | copy-start | bytes 1769476
  118.2 123.7 %all-to-all-start = ((bf16[4,2,663552]{2,1,0:T(2,128)(2,1)}), bf16[4,2,663552]{2,1,0:T(2,128)(2,1)}, u32[]{:S(2)}, u32[]{:S(2)}) async-start(bf16[4,2,663552]{2,1,0:T(2,128)(2,1)} %reshape.138), calls=%async_computation | async-start | bytes 21233664 | tf_op jit(solution)/shard_map/all_to_all | solution.py:31
  242.0 248.7 %all-to-all-start.2 = ((bf16[4,2,663552]{2,1,0:T(2,128)(2,1)}), bf16[4,2,663552]{2,1,0:T(2,128)(2,1)}, u32[]{:S(2)}, u32[]{:S(2)}) async-start(bf16[4,2,663552]{2,1,0:T(2,128)(2,1)} %reshape.136), calls=%async_computation.2 | async-start | bytes 21233664 | tf_op jit(solution)/shard_map/all_to_all | solution.py:38
  353.9 11.7 copy-start.4
  365.6 25.7 %copy-start.2 = (f32[192,48,96]{0,2,1:T(8,128)S(1)}, f32[192,48,96]{0,2,1:T(8,128)}, u32[]{:S(2)}) copy-start(f32[192,48,96]{0,2,1:T(8,128)} %copy.72) | copy-start | bytes 10616836
  365.6 25.7 %copy-start.6 = (f32[5]{0:T(128)S(1)}, f32[5]{0:T(128)}, u32[]{:S(2)}) copy-start(f32[5]{0:T(128)} %param.15) | copy-start | bytes 64
  490.6 174.8 %all-to-all-start.1 = ((bf16[5,192,48,96]{3,2,0,1:T(8,128)(2,1)}), bf16[5,192,48,96]{3,2,0,1:T(8,128)(2,1)}, u32[]{:S(2)}, u32[]{:S(2)}) async-start(bf16[5,192,48,96]{3,2,0,1:T(8,128)(2,1)} %copy.76), calls=%async_computation.1 | async-start | bytes 23592960 | tf_op jit(solution)/shard_map/all_to_all | solution.py:36
  591.4 11.5 copy-start.5
  665.4 6.4 copy-start.7
  665.4 6.4 copy-start.3
  665.4 263.3 %all-to-all-start.3 = ((bf16[5,48,192,96]{3,1,0,2:T(8,128)(2,1)}), bf16[5,48,192,96]{3,1,0,2:T(8,128)(2,1)}, u32[]{:S(2)}, u32[]{:S(2)}) async-start(bf16[5,48,192,96]{3,1,0,2:T(8,128)(2,1)} %copy.86), calls=%async_computation.3 | async-start | bytes 23592960 | tf_op jit(solution)/shard_map/all_to_all | solution.py:43
  671.8 707.8 %reduce-scatter.4.cloned.1.call-start = ((), (), s32[]{:S(2)}) async-start(), calls=%async_computation.5 | async-start | bytes 26542080
  1408.0 30.7 %copy-start.1 = (bf16[2,384,384]{2,1,0:T(8,128)(2,1)S(1)}, bf16[2,384,384]{2,1,0:T(8,128)(2,1)}, u32[]{:S(2)}) copy-start(bf16[2,384,384]{2,1,0:T(8,128)(2,1)} %param.16) | copy-start | bytes 1769476
Sparse Core Ops, SparseCore 0:
  1181.3 198.2 reduce-scatter.3
where the time goes:
time: 1460 us; the launch traced here: 1450 us
  local copies, waits for them, and re-layouts  738 us (51%)
  waiting for transfers between devices  467 us (32%)
  other arithmetic  123 us (8%)
  matrix products  67.9 us (5%)
  starting transfers between devices  35.8 us (2%)
    unnamed x24, local copies, waits for them, and re-layouts  421 us
    unnamed x2, waiting for transfers between devices  198 us
    all_to_all x1, waiting for transfers between devices, on_device(): lax.all_to_all(term_z, 'col', split_axis=2, concat_axis=3, tiled=True)  187 us
    all_to_all x1, waiting for transfers between devices, on_device(): lax.all_to_all(stack_z, 'col', split_axis=3, concat_axis=2, tiled=True)  62.1 us
    convert_element_type x2, local copies, waits for them, and re-layouts, on_device(): back_y.astype(jnp.float32)  40.6 us
    mul x1, other arithmetic, on_device(): section_out[0].astype(jnp.float32)[None]  38.7 us
    concatenate x1, local copies, waits for them, and re-layouts, on_device(): stack_z = jnp.concatenate([flat_state, advect_z[None]], axis=0)  37.9 us
    concatenate x1, local copies, waits for them, and re-layouts, on_device(): stack_y = jnp.concatenate([flat_state, advect_y[None]], axis=0)  37.9 us
  transfers between devices with their start and end apart: 5, of which 4 were waited for; matrix products, arithmetic and copies ran while one was open for 35% of the time, Pallas kernels for 0%

commit v1 on v0

v1 whole, which is shorter than its diff:
```python
import jax
import jax.numpy as jnp
from jax import lax
from jax.experimental import pallas as pl
from jax.experimental.pallas import tpu as pltpu
from jax.sharding import PartitionSpec as P

step_size = 0.25
F32, BF16 = jnp.float32, jnp.bfloat16
VMEM_BYTES = 52 * 1024 * 1024
SMEM = pl.BlockSpec(memory_space=pltpu.SMEM)


def params():
    return pltpu.CompilerParams(vmem_limit_bytes=VMEM_BYTES)


def cost(flops, nbytes):
    return pl.CostEstimate(flops=flops, bytes_accessed=nbytes, transcendentals=0)


def xy_kernel(coef, state, forcing, adv_x, adv_y, lines, mat_x, mat_y, out):
    _, ny, zb, nx = state.shape
    rows = ny * zb
    c = coef[pl.program_id(1)]
    own = state[...].reshape(rows, nx)
    gx = jnp.dot(own, mat_x[...], preferred_element_type=F32)
    total = c * gx[:, nx:] - adv_x[...].reshape(rows, nx).astype(F32) * gx[:, :nx]
    gy = jnp.dot(mat_y[...], lines[...].reshape(mat_y.shape[1], nx), preferred_element_type=F32)
    total += c * gy[rows:] - adv_y[...].reshape(rows, nx).astype(F32) * gy[:rows]
    total += forcing[...].reshape(rows, nx).astype(F32)
    out[...] = (own.astype(F32) + step_size * total).reshape(out.shape)


def z_kernel(v, coef, lines, adv, mat_z, out):
    n, yb, nz, nx = lines.shape
    full = n * nz
    c = coef[v]
    for y in range(yb):
        g = jnp.dot(mat_z[...], lines[:, y].reshape(full, nx), preferred_element_type=F32)
        term = c * g[full:] - adv[:, y].reshape(full, nx).astype(F32) * g[:full]
        out[:, y] = term.astype(BF16).reshape(n, nz, nx)


def combine_kernel(me, pre, back, *refs):
    section, own, send = refs[-3:]
    total = (pre[0] + step_size * back[...].astype(F32)).astype(BF16)
    section[0] = total
    part = own.shape[-1]
    n = total.shape[-1] // part
    pieces = [total[..., k * part : (k + 1) * part] for k in range(n)]

    @pl.when(me[0] == 0)
    def _():
        own[...] = pieces[0]
        for s in range(1, n):
            send[s - 1] = pieces[s]

    for p in range(1, n):
        @pl.when(me[0] == p)
        def _(p=p):
            own[...] = pieces[p]
            for s in range(1, n):
                send[s - 1] = pieces[(p + s) % n]


def sketch_kernel(mix, own, got, *refs):
    out = refs[-1]
    for g in range(out.shape[0]):
        total = (own[...].astype(F32) * mix[0, g]).astype(BF16).astype(F32)
        for s in range(got.shape[0]):
            total += (got[s].astype(F32) * mix[s + 1, g]).astype(BF16).astype(F32)
        out[g, 0] = total.astype(BF16)


def on_device(flow_state, forcing, advect_x, advect_y, advect_z, diffusivity, deriv_x, deriv_y, deriv_z, test_mix):
    frc_dev, nvars, ny, nz, nx = flow_state.shape
    assert frc_dev == 1
    n_row, n_col, n_probe = lax.axis_size("row"), lax.axis_size("col"), lax.axis_size("probe")
    columns = test_mix.shape[1]
    part = nx // n_probe
    yb = -(-ny // n_col)
    spare = yb * n_col - ny
    state, force = flow_state[0], forcing[0]
    probe = lax.axis_index("probe")

    def exchange(block):
        return lax.all_to_all(block, "col", split_axis=0, concat_axis=0)

    def divided(block):
        if spare:
            block = jnp.pad(block, ((0, spare), (0, 0), (0, 0)))
        return block.reshape(n_col, yb, nz, nx)

    adv_z = exchange(divided(advect_z))
    lines_z = [exchange(divided(state[v])) for v in range(nvars)]
    lines_y = lax.all_gather(state, "row")

    zb = 16 if nz % 16 == 0 else nz
    own_rows = lax.dynamic_slice_in_dim(deriv_y, lax.axis_index("row") * ny, ny, 1)
    own_rows = own_rows.reshape(2 * ny, n_row * ny)
    tall, wide = 2 * ny * zb, n_row * ny * zb
    spread_rows = (jnp.arange(tall)[:, None] // zb == jnp.arange(2 * ny)[None]).astype(BF16)
    spread_cols = (jnp.arange(n_row * ny)[:, None] == jnp.arange(wide)[None] // zb).astype(BF16)
    mat_y = jnp.dot(spread_rows, own_rows, preferred_element_type=BF16)
    mat_y = jnp.dot(mat_y, spread_cols, preferred_element_type=BF16)
    same_z = jnp.arange(tall)[:, None] % zb == jnp.arange(wide)[None] % zb
    mat_y = jnp.where(same_z, mat_y, jnp.zeros((), BF16))
    mat_x = deriv_x.reshape(2 * nx, nx).T
    mat_z = deriv_z.reshape(2 * n_col * nz, n_col * nz)

    block = ny * nz * nx
    one = pl.BlockSpec((1, ny, zb, nx), lambda z, v: (v, 0, z, 0))
    adv = pl.BlockSpec((ny, zb, nx), lambda z, v: (0, z, 0))
    pre = pl.pallas_call(
        xy_kernel,
        grid=(nz // zb, nvars),
        in_specs=[
            SMEM, one, one, adv, adv,
            pl.BlockSpec((n_row, 1, ny, zb, nx), lambda z, v: (0, v, 0, z, 0)),
            pl.BlockSpec(mat_x.shape, lambda z, v: (0, 0), pipeline_mode=pl.Buffered(1)),
            pl.BlockSpec(mat_y.shape, lambda z, v: (0, 0), pipeline_mode=pl.Buffered(1)),
        ],
        out_specs=one,
        out_shape=jax.ShapeDtypeStruct(state.shape, F32),
        compiler_params=params(),
        cost_estimate=cost(nvars * block * (4 * nx + 4 * n_row * ny * zb), nvars * block * (8 + 2 * n_row)),
        name="xy_terms",
    )(diffusivity, state, force, advect_x, advect_y, lines_y, mat_x, mat_y)

    ys = next(k for k in (4, 3, 2, 1) if yb % k == 0)
    z_spec = pl.BlockSpec((n_col, ys, nz, nx), lambda y: (0, y, 0, 0))
    back = []
    for v in range(nvars):
        term = pl.pallas_call(
            lambda *refs, v=v: z_kernel(v, *refs),
            grid=(yb // ys,),
            in_specs=[SMEM, z_spec, z_spec, pl.BlockSpec(mat_z.shape, lambda y: (0, 0))],
            out_specs=z_spec,
            out_shape=jax.ShapeDtypeStruct((n_col, yb, nz, nx), BF16),
            compiler_params=params(),
            cost_estimate=cost(block * 4 * n_col * nz, block * 6),
            name="z_terms",
        )(diffusivity, lines_z[v], adv_z, mat_z)
        back.append(exchange(term).reshape(n_col * yb, nz, nx)[:ny])

    yc = next(k for k in (12, 8, 6, 4, 3, 2, 1) if ny % k == 0)
    mix = jnp.stack([test_mix[lax.rem(probe - s + n_probe, n_probe)] for s in range(n_probe)])
    me = probe.reshape(1)
    section, owns, gots = None, [], []
    any_spec = pl.BlockSpec(memory_space=pl.ANY)
    for v in range(nvars):
        carried = [] if section is None else [section]
        section, own, send = pl.pallas_call(
            combine_kernel,
            grid=(ny // yc,),
            in_specs=[
                SMEM,
                pl.BlockSpec((1, yc, nz, nx), lambda y, v=v: (v, y, 0, 0)),
                pl.BlockSpec((yc, nz, nx), lambda y: (y, 0, 0)),
            ] + [any_spec] * len(carried),
            out_specs=[
                pl.BlockSpec((1, yc, nz, nx), lambda y, v=v: (v, y, 0, 0)),
                pl.BlockSpec((yc, nz, part), lambda y: (y, 0, 0)),
                pl.BlockSpec((n_probe - 1, yc, nz, part), lambda y: (0, y, 0, 0)),
            ],
            out_shape=[
                jax.ShapeDtypeStruct(state.shape, BF16),
                jax.ShapeDtypeStruct((ny, nz, part), BF16),
                jax.ShapeDtypeStruct((n_probe - 1, ny, nz, part), BF16),
            ],
            input_output_aliases={3: 0} if carried else {},
            compiler_params=params(),
            cost_estimate=cost(block * 2, block * 10),
            name="combine",
        )(me, pre, back[v], *carried)
        got = [
            lax.ppermute(send[s - 1], "probe", [(p, (p + s) % n_probe) for p in range(n_probe)])
            for s in range(1, n_probe)
        ]
        owns.append(own)
        gots.append(got[0][None] if n_probe == 2 else jnp.stack(got))

    sketch = None
    for v in range(nvars):
        carried = [] if sketch is None else [sketch]
        sketch = pl.pallas_call(
            sketch_kernel,
            grid=(ny // yc,),
            in_specs=[
                SMEM,
                pl.BlockSpec((yc, nz, part), lambda y: (y, 0, 0)),
                pl.BlockSpec((n_probe - 1, yc, nz, part), lambda y: (0, y, 0, 0)),
            ] + [any_spec] * len(carried),
            out_specs=pl.BlockSpec((columns, 1, yc, nz, part), lambda y, v=v: (0, v, y, 0, 0)),
            out_shape=jax.ShapeDtypeStruct((columns, nvars, ny, nz, part), BF16),
            input_output_aliases={3: 0} if carried else {},
            compiler_params=params(),
            cost_estimate=cost(block * 4, block * 4),
            name="sketch_columns",
        )(mix, owns[v], gots[v], *carried)
    return (section[None], sketch)


def solution(mesh):
    placed = (
        P("probe", None, "row", "col", None),
        P("probe", None, "row", "col", None),
        P("row", "col", None),
        P("row", "col", None),
        P("row", "col", None),
        P(),
        P(),
        P(),
        P(),
        P(),
    )
    return jax.shard_map(
        on_device,
        mesh=mesh,
        in_specs=placed,
        out_specs=(P("probe", None, "row", "col", None), P(None, None, "row", "col", "probe")),
        check_vma=False,
    )
```

time: 1460 us -> 709 us (0.49)
  local copies, waits for them, and re-layouts: 738 us -> 7.42 us
  blocking collectives: 0 us -> 222 us
  waiting for transfers between devices: 467 us -> 258 us
  Pallas kernels: 0 us -> 167 us
  other arithmetic: 123 us -> 0.02 us
  matrix products: 67.9 us -> 5.96 us
    unnamed x24 -> x22, local copies, waits for them, and re-layouts: 421 us -> 2.23 us
    all_to_all x0 -> x5, blocking collectives: none -> 222 us  [exchange(): return lax.all_to_all(block, 'col', split_axis=0, concat_axis=0)]
    unnamed x2 -> x1, waiting for transfers between devices: 198 us -> 0.68 us
    pallas_call x0 -> x16, Pallas kernels: none -> 167 us  [the longest x1 97.4 us: on_device(): pl.pallas_call(xy_kernel, grid=(nz // zb, nvars), in_specs=[SMEM, one, on...]
    convert_element_type x10 -> x0, local copies, waits for them, and re-layouts: 128 us -> none  [the longest x2 40.6 us: on_device(): back_y.astype(jnp.float32)]
    all_to_all x4 -> x6, waiting for transfers between devices: 268 us -> 173 us  [exchange(): return lax.all_to_all(block, 'col', split_axis=0, concat_axis=0)]
    all_to_all x4 -> x0, local copies, waits for them, and re-layouts: 85.8 us -> none  [the longest x1 36.1 us: on_device(): lax.all_to_all(stack_y, 'row', split_axis=3, concat_axis=1, tiled=True)]
    ppermute x0 -> x5, waiting for transfers between devices: none -> 83.5 us  [on_device(): lax.ppermute(send[s - 1], 'probe', [(p, (p + s) % n_probe) for p in range...]
  transfers between devices with their start and end apart: 5 -> 12, of which waited for: 4 -> 10; matrix products, arithmetic and copies ran while one was open for 35% -> 2% of each run, Pallas kernels for 0% -> 23%
where the time goes in v1:
time: 709 us; the launch traced here: 707 us
  waiting for transfers between devices  258 us (36%)
  blocking collectives  222 us (31%)
  Pallas kernels  167 us (24%)
  starting transfers between devices  32.3 us (5%)
  between operations  14.2 us (2%)
  local copies, waits for them, and re-layouts  7.42 us (1%)
    all_to_all x5, blocking collectives, exchange(): return lax.all_to_all(block, 'col', split_axis=0, concat_axis=0)  222 us
    all_to_all x6, waiting for transfers between devices, exchange(): return lax.all_to_all(block, 'col', split_axis=0, concat_axis=0)  173 us
    pallas_call x1, Pallas kernels, on_device(): pl.pallas_call(xy_kernel, grid=(nz // zb, nvars), in_specs=[SMEM, one, on...  97.4 us
    ppermute x5, waiting for transfers between devices, on_device(): lax.ppermute(send[s - 1], 'probe', [(p, (p + s) % n_probe) for p in range...  83.5 us
    all_to_all x6, starting transfers between devices, exchange(): return lax.all_to_all(block, 'col', split_axis=0, concat_axis=0)  26.7 us
    pallas_call x5, Pallas kernels, on_device(): pl.pallas_call(combine_kernel, grid=(ny // yc,), in_specs=[SMEM, pl.Block...  24.9 us
    pallas_call x5, Pallas kernels, on_device(): pl.pallas_call(lambda *refs, v=v: z_kernel(v, *refs), grid=(yb // ys,), i...  23.6 us
    pallas_call x5, Pallas kernels, on_device(): pl.pallas_call(sketch_kernel, grid=(ny // yc,), in_specs=[SMEM, pl.BlockS...  21.5 us
  transfers between devices with their start and end apart: 12, of which 10 were waited for; matrix products, arithmetic and copies ran while one was open for 2% of the time, Pallas kernels for 23%

profile of v1, /device:TPU:0, one launch (start us, length us, event | category | flops | bytes accessed | tf_op | source)
XLA Modules:
  0.0 707.0 jit_solution(9582166438938820737)
XLA Ops:
  7.9 4.9 fusion.15
  12.8 47.5 %all_to_all.55.refs_1_ = bf16[4,12,48,384]{3,2,1,0:T(8,128)(2,1)} all-to-all(bf16[4,12,48,384]{3,2,1,0:T(8,128)(2,1)S(1)} %bitcast.41), channel_id=1, replica_groups=mesh['probe'=2,'row'=4,'col'=4] {'col'}, dimensions={0} | all-to-all | bytes 3538944 | tf_op jit(solution)/shard_map/all_to_all | solution.py:88
  60.3 43.9 %all_to_all.56.refs_2_ = bf16[4,12,48,384]{3,2,1,0:T(8,128)(2,1)} all-to-all(bf16[4,12,48,384]{3,2,1,0:T(8,128)(2,1)S(1)} %bitcast.42), channel_id=1, replica_groups=mesh['probe'=2,'row'=4,'col'=4] {'col'}, dimensions={0} | all-to-all | bytes 3538944 | tf_op jit(solution)/shard_map/all_to_all | solution.py:88
  104.2 43.6 %all_to_all.57.refs_1_ = bf16[4,12,48,384]{3,2,1,0:T(8,128)(2,1)} all-to-all(bf16[4,12,48,384]{3,2,1,0:T(8,128)(2,1)S(1)} %bitcast.40), channel_id=1, replica_groups=mesh['probe'=2,'row'=4,'col'=4] {'col'}, dimensions={0} | all-to-all | bytes 3538944 | tf_op jit(solution)/shard_map/all_to_all | solution.py:88
  147.8 43.6 %all_to_all.58.refs_1_ = bf16[4,12,48,384]{3,2,1,0:T(8,128)(2,1)} all-to-all(bf16[4,12,48,384]{3,2,1,0:T(8,128)(2,1)S(1)} %bitcast.39), channel_id=1, replica_groups=mesh['probe'=2,'row'=4,'col'=4] {'col'}, dimensions={0} | all-to-all | bytes 3538944 | tf_op jit(solution)/shard_map/all_to_all | solution.py:88
  191.4 43.6 %all_to_all.59.refs_1_ = bf16[4,12,48,384]{3,2,1,0:T(8,128)(2,1)} all-to-all(bf16[4,12,48,384]{3,2,1,0:T(8,128)(2,1)S(1)} %bitcast.38), channel_id=1, replica_groups=mesh['probe'=2,'row'=4,'col'=4] {'col'}, dimensions={0} | all-to-all | bytes 3538944 | tf_op jit(solution)/shard_map/all_to_all | solution.py:88
  239.6 4.7 z_terms.6
  244.3 35.7 %all-to-all-done.9.refs_1_ = bf16[4,12,48,384]{3,2,1,0:T(8,128)(2,1)} async-done(((bf16[4,12,48,384]{3,2,1,0:T(8,128)(2,1)}), bf16[4,12,48,384]{3,2,1,0:T(8,128)(2,1)}, u32[]{:S(2)}, u32[]{:S(2)}) %all-to-all-start.9) | async-done | bytes 1769504 | tf_op jit(solution)/shard_map/all_to_all | solution.py:88
  284.5 4.7 z_terms.7
  289.2 36.0 %all-to-all-done.4 = bf16[4,12,48,384]{3,2,1,0:T(8,128)(2,1)} async-done(((bf16[4,12,48,384]{3,2,1,0:T(8,128)(2,1)}), bf16[4,12,48,384]{3,2,1,0:T(8,128)(2,1)}, u32[]{:S(2)}, u32[]{:S(2)}) %all-to-all-start.4) | async-done | bytes 1769504 | tf_op jit(solution)/shard_map/all_to_all | solution.py:88
  334.3 36.0 %all-to-all-done.6 = bf16[4,12,48,384]{3,2,1,0:T(8,128)(2,1)} async-done(((bf16[4,12,48,384]{3,2,1,0:T(8,128)(2,1)}), bf16[4,12,48,384]{3,2,1,0:T(8,128)(2,1)}, u32[]{:S(2)}, u32[]{:S(2)}) %all-to-all-start.6) | async-done | bytes 1769504 | tf_op jit(solution)/shard_map/all_to_all | solution.py:88
  379.5 36.0 %all-to-all-done.8 = bf16[4,12,48,384]{3,2,1,0:T(8,128)(2,1)} async-done(((bf16[4,12,48,384]{3,2,1,0:T(8,128)(2,1)}), bf16[4,12,48,384]{3,2,1,0:T(8,128)(2,1)}, u32[]{:S(2)}, u32[]{:S(2)}) %all-to-all-start.8) | async-done | bytes 1769504 | tf_op jit(solution)/shard_map/all_to_all | solution.py:88
  420.2 6.0 compare_select_fusion.mat_y
  430.8 29.7 %all-to-all-done.10 = bf16[4,12,48,384]{3,2,1,0:T(8,128)(2,1)} async-done(((bf16[4,12,48,384]{3,2,1,0:T(8,128)(2,1)}), bf16[4,12,48,384]{3,2,1,0:T(8,128)(2,1)}, u32[]{:S(2)}, u32[]{:S(2)}) %all-to-all-start.10) | async-done | bytes 1769504 | tf_op jit(solution)/shard_map/all_to_all | solution.py:88
  465.2 97.4 %xy_terms.1.pre = f32[5,48,48,384]{3,2,1,0:T(8,128)} custom-call(f32[5]{0:T(128)S(1)} %copy-done.7, bf16[5,48,48,384]{3,2,1,0:T(8,128)(2,1)} %bitcast.37, bf16[5,48,48,384]{3,2,1,0:T(8,128)(2,1)} %bitcast.45, bf16[48,48,384]{2,1,0:T(8,128)(2,1)} %adv_x.1, bf16[48,48,384]{2,1,0:T(8,128)(2,1)} %adv_y.1, ...), custom_call_target="tpu_custom_call" | custom-call | flops 61152952320 | bytes 70778880 | tf_op jit(solution)/shard_map/xy_terms/pallas_call | solution.py:115
  562.5 5.0 combine.5
  569.0 5.0 combine.6
  574.5 5.0 combine.7
  581.0 5.0 combine.8
  587.6 5.0 combine.9
  601.0 21.0 %collective-permute-done.3 = bf16[48,48,192]{2,1,0:T(8,128)(2,1)} collective-permute-done((bf16[48,48,192]{2,1,0:T(8,128)(2,1)}, bf16[48,48,192]{2,1,0:T(8,128)(2,1)}, u32[]{:S(2)}, u32[]{:S(2)}) %collective-permute-start.3) | collective-permute-done | bytes 884768 | tf_op jit(solution)/shard_map/ppermute | solution.py:178
  626.2 21.0 %collective-permute-done.2 = bf16[48,48,192]{2,1,0:T(8,128)(2,1)} collective-permute-done((bf16[48,48,192]{2,1,0:T(8,128)(2,1)}, bf16[48,48,192]{2,1,0:T(8,128)(2,1)}, u32[]{:S(2)}, u32[]{:S(2)}) %collective-permute-start.2) | collective-permute-done | bytes 884768 | tf_op jit(solution)/shard_map/ppermute | solution.py:178
  651.6 20.9 %collective-permute-done.1 = bf16[48,48,192]{2,1,0:T(8,128)(2,1)} collective-permute-done((bf16[48,48,192]{2,1,0:T(8,128)(2,1)}, bf16[48,48,192]{2,1,0:T(8,128)(2,1)}, u32[]{:S(2)}, u32[]{:S(2)}) %collective-permute-start.1) | collective-permute-done | bytes 884768 | tf_op jit(solution)/shard_map/ppermute | solution.py:178
  676.9 18.9 %collective-permute-done = bf16[48,48,192]{2,1,0:T(8,128)(2,1)} collective-permute-done((bf16[48,48,192]{2,1,0:T(8,128)(2,1)}, bf16[48,48,192]{2,1,0:T(8,128)(2,1)}, u32[]{:S(2)}, u32[]{:S(2)}) %collective-permute-start) | collective-permute-done | bytes 884768 | tf_op jit(solution)/shard_map/ppermute | solution.py:178
  (52 shorter events, 72.7 us)
Async XLA Ops:
  7.2 413.0 %copy-start = (bf16[2,192,192]{2,1,0:T(8,128)(2,1)S(1)}, bf16[2,192,192]{2,1,0:T(8,128)(2,1)}, u32[]{:S(2)}) copy-start(bf16[2,192,192]{2,1,0:T(8,128)(2,1)} %param.17) | copy-start | bytes 442372
  7.2 458.0 %all-gather.2.cloned.1.call-start = ((), (), s32[]{:S(2)}) async-start(), calls=%async_computation.11 | async-start | bytes 44236800 | tf_op jit(solution)/shard_map/all_gather | solution.py:97
  12.8 47.5 %copy-start.8 = (bf16[48,48,384]{2,1,0:T(8,128)(2,1)S(1)}, bf16[48,48,384]{2,1,0:T(8,128)(2,1)}, u32[]{:S(2)}) copy-start(bf16[48,48,384]{2,1,0:T(8,128)(2,1)} %param.14) | copy-start | bytes 5308420
  235.0 4.6 copy-start.2
  235.0 4.6 copy-start.7
  235.0 45.0 %all-to-all-start.9 = ((bf16[4,12,48,384]{3,2,1,0:T(8,128)(2,1)}), bf16[4,12,48,384]{3,2,1,0:T(8,128)(2,1)}, u32[]{:S(2)}, u32[]{:S(2)}) async-start(bf16[4,12,48,384]{3,2,1,0:T(8,128)(2,1)} %bitcast.16), calls=%async_computation.9 | async-start | bytes 3538944 | tf_op jit(solution)/shard_map/all_to_all | solution.py:88
  280.0 45.1 %all-to-all-start.4 = ((bf16[4,12,48,384]{3,2,1,0:T(8,128)(2,1)}), bf16[4,12,48,384]{3,2,1,0:T(8,128)(2,1)}, u32[]{:S(2)}, u32[]{:S(2)}) async-start(bf16[4,12,48,384]{3,2,1,0:T(8,128)(2,1)} %z_terms.6), calls=%async_computation.4 | async-start | bytes 3538944 | tf_op jit(solution)/shard_map/all_to_all | solution.py:88
  325.2 45.1 %all-to-all-start.6 = ((bf16[4,12,48,384]{3,2,1,0:T(8,128)(2,1)}), bf16[4,12,48,384]{3,2,1,0:T(8,128)(2,1)}, u32[]{:S(2)}, u32[]{:S(2)}) async-start(bf16[4,12,48,384]{3,2,1,0:T(8,128)(2,1)} %z_terms.7), calls=%async_computation.6 | async-start | bytes 3538944 | tf_op jit(solution)/shard_map/all_to_all | solution.py:88
  370.3 45.1 %all-to-all-start.8 = ((bf16[4,12,48,384]{3,2,1,0:T(8,128)(2,1)}), bf16[4,12,48,384]{3,2,1,0:T(8,128)(2,1)}, u32[]{:S(2)}, u32[]{:S(2)}) async-start(bf16[4,12,48,384]{3,2,1,0:T(8,128)(2,1)} %z_terms.8), calls=%async_computation.8 | async-start | bytes 3538944 | tf_op jit(solution)/shard_map/all_to_all | solution.py:88
  379.4 40.4 %copy-start.9 = (bf16[2,384,384]{2,1,0:T(8,128)(2,1)S(1)}, bf16[2,384,384]{2,1,0:T(8,128)(2,1)}, u32[]{:S(2)}) copy-start(bf16[2,384,384]{2,1,0:T(8,128)(2,1)} %param.16) | copy-start | bytes 1769476
  415.5 45.1 %all-to-all-start.10 = ((bf16[4,12,48,384]{3,2,1,0:T(8,128)(2,1)}), bf16[4,12,48,384]{3,2,1,0:T(8,128)(2,1)}, u32[]{:S(2)}, u32[]{:S(2)}) async-start(bf16[4,12,48,384]{3,2,1,0:T(8,128)(2,1)} %z_terms.9), calls=%async_computation.10 | async-start | bytes 3538944 | tf_op jit(solution)/shard_map/all_to_all | solution.py:88
  460.6 127.0 %all-to-all-start.2 = ((bf16[4,12,48,384]{3,2,1,0:T(8,128)(2,1)}), bf16[4,12,48,384]{3,2,1,0:T(8,128)(2,1)}, u32[]{:S(2)}, u32[]{:S(2)}) async-start(bf16[4,12,48,384]{3,2,1,0:T(8,128)(2,1)} %z_terms.5), calls=%async_computation.2 | async-start | bytes 3538944 | tf_op jit(solution)/shard_map/all_to_all | solution.py:88
  567.5 29.2 %collective-permute-start.4 = (bf16[48,48,192]{2,1,0:T(8,128)(2,1)}, bf16[48,48,192]{2,1,0:T(8,128)(2,1)}, u32[]{:S(2)}, u32[]{:S(2)}) collective-permute-start(bf16[48,48,192]{2,1,0:T(8,128)(2,1)} %bitcast.46), channel_id=1, source_target_pairs={{0,16},{16,0},{1,17},{17,1},{2,18},{18,2},{3,19},{19,3},{4,20},{20... | collective-permute-start | bytes 2654216 | tf_op jit(solution)/shard_map/ppermute | solution.py:178
  574.0 48.0 %collective-permute-start.3 = (bf16[48,48,192]{2,1,0:T(8,128)(2,1)}, bf16[48,48,192]{2,1,0:T(8,128)(2,1)}, u32[]{:S(2)}, u32[]{:S(2)}) collective-permute-start(bf16[48,48,192]{2,1,0:T(8,128)(2,1)} %bitcast.47), channel_id=1, source_target_pairs={{0,16},{16,0},{1,17},{17,1},{2,18},{18,2},{3,19},{19,3},{4,20},{20... | collective-permute-start | bytes 2654216 | tf_op jit(solution)/shard_map/ppermute | solution.py:178
  579.5 67.8 %collective-permute-start.2 = (bf16[48,48,192]{2,1,0:T(8,128)(2,1)}, bf16[48,48,192]{2,1,0:T(8,128)(2,1)}, u32[]{:S(2)}, u32[]{:S(2)}) collective-permute-start(bf16[48,48,192]{2,1,0:T(8,128)(2,1)} %bitcast.48), channel_id=1, source_target_pairs={{0,16},{16,0},{1,17},{17,1},{2,18},{18,2},{3,19},{19,3},{4,20},{20... | collective-permute-start | bytes 2654216 | tf_op jit(solution)/shard_map/ppermute | solution.py:178
  585.9 1.1 copy-start.3
  587.0 85.5 %collective-permute-start.1 = (bf16[48,48,192]{2,1,0:T(8,128)(2,1)}, bf16[48,48,192]{2,1,0:T(8,128)(2,1)}, u32[]{:S(2)}, u32[]{:S(2)}) collective-permute-start(bf16[48,48,192]{2,1,0:T(8,128)(2,1)} %bitcast.49), channel_id=1, source_target_pairs={{0,16},{16,0},{1,17},{17,1},{2,18},{18,2},{3,19},{19,3},{4,20},{20... | collective-permute-start | bytes 2654216 | tf_op jit(solution)/shard_map/ppermute | solution.py:178
  587.6 7.6 %copy-start.10 = (f32[2,2]{1,0:T(2,128)S(1)}, f32[2,2]{1,0:T(2,128)}, u32[]{:S(2)}) copy-start(f32[2,2]{1,0:T(2,128)} %param.19) | copy-start | bytes 52
  592.5 1.1 copy-start.5
  593.6 102.2 %collective-permute-start = (bf16[48,48,192]{2,1,0:T(8,128)(2,1)}, bf16[48,48,192]{2,1,0:T(8,128)(2,1)}, u32[]{:S(2)}, u32[]{:S(2)}) collective-permute-start(bf16[48,48,192]{2,1,0:T(8,128)(2,1)} %bitcast.50), channel_id=1, source_target_pairs={{0,16},{16,0},{1,17},{17,1},{2,18},{18,2},{3,19},{19,3},{4,20},{20... | collective-permute-start | bytes 2654216 | tf_op jit(solution)/shard_map/ppermute | solution.py:178
  647.3 25.3 %copy-start.4 = (bf16[48,48,192]{2,1,0:T(8,128)(2,1)S(1)}, bf16[48,48,192]{2,1,0:T(8,128)(2,1)}, u32[]{:S(2)}) copy-start(bf16[48,48,192]{2,1,0:T(8,128)(2,1)} %copy-done.3) | copy-start | bytes 2654212
  672.6 23.3 %copy-start.6 = (bf16[48,48,192]{2,1,0:T(8,128)(2,1)S(1)}, bf16[48,48,192]{2,1,0:T(8,128)(2,1)}, u32[]{:S(2)}) copy-start(bf16[48,48,192]{2,1,0:T(8,128)(2,1)} %copy-done.5) | copy-start | bytes 2654212
  695.9 4.3 copy-start.1
Sparse Core Ops, SparseCore 0:
  9.6 216.8 all-gather.1

commit v2 on v1

--- a/solution.py
+++ b/solution.py
@@ -19,10 +19,11 @@
     return pl.CostEstimate(flops=flops, bytes_accessed=nbytes, transcendentals=0)
 
 
-def xy_kernel(coef, state, forcing, adv_x, adv_y, lines, mat_x, mat_y, out):
+def xy_kernel(coef, state, forcing, adv_x, adv_y, lines, mat_x, mat_y, *refs):
+    out = refs[-1]
     _, ny, zb, nx = state.shape
     rows = ny * zb
-    c = coef[pl.program_id(1)]
+    c = coef[0]
     own = state[...].reshape(rows, nx)
     gx = jnp.dot(own, mat_x[...], preferred_element_type=F32)
     total = c * gx[:, nx:] - adv_x[...].reshape(rows, nx).astype(F32) * gx[:, :nx]
@@ -32,10 +33,11 @@
     out[...] = (own.astype(F32) + step_size * total).reshape(out.shape)
 
 
-def z_kernel(v, coef, lines, adv, mat_z, out):
+def z_kernel(coef, lines, adv, mat_z, *refs):
+    out = refs[-1]
     n, yb, nz, nx = lines.shape
     full = n * nz
-    c = coef[v]
+    c = coef[0]
     for y in range(yb):
         g = jnp.dot(mat_z[...], lines[:, y].reshape(full, nx), preferred_element_type=F32)
         term = c * g[full:] - adv[:, y].reshape(full, nx).astype(F32) * g[:full]
@@ -44,7 +46,7 @@
 
 def combine_kernel(me, pre, back, *refs):
     section, own, send = refs[-3:]
-    total = (pre[0] + step_size * back[...].astype(F32)).astype(BF16)
+    total = (pre[...] + step_size * back[...].astype(F32)).astype(BF16)
     section[0] = total
     part = own.shape[-1]
     n = total.shape[-1] // part
@@ -79,7 +81,8 @@
     n_row, n_col, n_probe = lax.axis_size("row"), lax.axis_size("col"), lax.axis_size("probe")
     columns = test_mix.shape[1]
     part = nx // n_probe
-    yb = -(-ny // n_col)
+    yb = -(-ny // (n_col * n_probe)) * n_probe
+    half = yb // n_probe
     spare = yb * n_col - ny
     state, force = flow_state[0], forcing[0]
     probe = lax.axis_index("probe")
@@ -92,7 +95,15 @@
             block = jnp.pad(block, ((0, spare), (0, 0), (0, 0)))
         return block.reshape(n_col, yb, nz, nx)
 
-    adv_z = exchange(divided(advect_z))
+    def passed(block, shift):
+        return lax.ppermute(block, "probe", [(p, (p + shift) % n_probe) for p in range(n_probe)])
+
+    mine = exchange(lax.dynamic_slice_in_dim(divided(advect_z), probe * half, half, 1))
+    adv_z = jnp.zeros((n_col, yb, nz, nx), BF16)
+    for s in range(n_probe):
+        share = passed(mine, s) if s else mine
+        source = lax.rem(probe - s + n_probe, n_probe)
+        adv_z = lax.dynamic_update_slice_in_dim(adv_z, share, source * half, 1)
     lines_z = [exchange(divided(state[v])) for v in range(nvars)]
     lines_y = lax.all_gather(state, "row")
 
@@ -110,57 +121,53 @@
     mat_z = deriv_z.reshape(2 * n_col * nz, n_col * nz)
 
     block = ny * nz * nx
-    one = pl.BlockSpec((1, ny, zb, nx), lambda z, v: (v, 0, z, 0))
-    adv = pl.BlockSpec((ny, zb, nx), lambda z, v: (0, z, 0))
-    pre = pl.pallas_call(
-        xy_kernel,
-        grid=(nz // zb, nvars),
-        in_specs=[
-            SMEM, one, one, adv, adv,
-            pl.BlockSpec((n_row, 1, ny, zb, nx), lambda z, v: (0, v, 0, z, 0)),
-            pl.BlockSpec(mat_x.shape, lambda z, v: (0, 0), pipeline_mode=pl.Buffered(1)),
-            pl.BlockSpec(mat_y.shape, lambda z, v: (0, 0), pipeline_mode=pl.Buffered(1)),
-        ],
-        out_specs=one,
-        out_shape=jax.ShapeDtypeStruct(state.shape, F32),
-        compiler_params=params(),
-        cost_estimate=cost(nvars * block * (4 * nx + 4 * n_row * ny * zb), nvars * block * (8 + 2 * n_row)),
-        name="xy_terms",
-    )(diffusivity, state, force, advect_x, advect_y, lines_y, mat_x, mat_y)
-
+    any_spec = pl.BlockSpec(memory_space=pl.ANY)
     ys = next(k for k in (4, 3, 2, 1) if yb % k == 0)
+    yc = next(k for k in (12, 8, 6, 4, 3, 2, 1) if ny % k == 0)
     z_spec = pl.BlockSpec((n_col, ys, nz, nx), lambda y: (0, y, 0, 0))
-    back = []
-    for v in range(nvars):
-        term = pl.pallas_call(
-            lambda *refs, v=v: z_kernel(v, *refs),
+    adv = pl.BlockSpec((ny, zb, nx), lambda z: (0, z, 0))
+    mix = jnp.stack([test_mix[lax.rem(probe - s + n_probe, n_probe)] for s in range(n_probe)])
+    me = probe.reshape(1)
+
+    def z_terms(v, after):
+        return pl.pallas_call(
+            z_kernel,
             grid=(yb // ys,),
-            in_specs=[SMEM, z_spec, z_spec, pl.BlockSpec(mat_z.shape, lambda y: (0, 0))],
+            in_specs=[SMEM, z_spec, z_spec, pl.BlockSpec(mat_z.shape, lambda y: (0, 0))] + [any_spec] * len(after),
             out_specs=z_spec,
             out_shape=jax.ShapeDtypeStruct((n_col, yb, nz, nx), BF16),
             compiler_params=params(),
             cost_estimate=cost(block * 4 * n_col * nz, block * 6),
             name="z_terms",
-        )(diffusivity, lines_z[v], adv_z, mat_z)
-        back.append(exchange(term).reshape(n_col * yb, nz, nx)[:ny])
-
-    yc = next(k for k in (12, 8, 6, 4, 3, 2, 1) if ny % k == 0)
-    mix = jnp.stack([test_mix[lax.rem(probe - s + n_probe, n_probe)] for s in range(n_probe)])
-    me = probe.reshape(1)
-    section, owns, gots = None, [], []
-    any_spec = pl.BlockSpec(memory_space=pl.ANY)
-    for v in range(nvars):
+        )(diffusivity[v : v + 1], lines_z[v], adv_z, mat_z, *after)
+
+    def xy_terms(v, after):
+        one = pl.BlockSpec((1, ny, zb, nx), lambda z: (v, 0, z, 0))
+        return pl.pallas_call(
+            xy_kernel,
+            grid=(nz // zb,),
+            in_specs=[
+                SMEM, one, one, adv, adv,
+                pl.BlockSpec((n_row, 1, ny, zb, nx), lambda z: (0, v, 0, z, 0)),
+                pl.BlockSpec(mat_x.shape, lambda z: (0, 0), pipeline_mode=pl.Buffered(1)),
+                pl.BlockSpec(mat_y.shape, lambda z: (0, 0), pipeline_mode=pl.Buffered(1)),
+            ] + [any_spec] * len(after),
+            out_specs=adv,
+            out_shape=jax.ShapeDtypeStruct((ny, nz, nx), F32),
+            compiler_params=params(),
+            cost_estimate=cost(block * (4 * nx + 4 * n_row * ny * zb), block * (8 + 2 * n_row)),
+            name="xy_terms",
+        )(diffusivity[v : v + 1], state, force, advect_x, advect_y, lines_y, mat_x, mat_y, *after)
+
+    def combine(v, pre, back, section):
         carried = [] if section is None else [section]
-        section, own, send = pl.pallas_call(
+        whole = pl.BlockSpec((yc, nz, nx), lambda y: (y, 0, 0))
+        return pl.pallas_call(
             combine_kernel,
             grid=(ny // yc,),
-            in_specs=[
-                SMEM,
-                pl.BlockSpec((1, yc, nz, nx), lambda y, v=v: (v, y, 0, 0)),
-                pl.BlockSpec((yc, nz, nx), lambda y: (y, 0, 0)),
-            ] + [any_spec] * len(carried),
+            in_specs=[SMEM, whole, whole] + [any_spec] * len(carried),
             out_specs=[
-                pl.BlockSpec((1, yc, nz, nx), lambda y, v=v: (v, y, 0, 0)),
+                pl.BlockSpec((1, yc, nz, nx), lambda y: (v, y, 0, 0)),
                 pl.BlockSpec((yc, nz, part), lambda y: (y, 0, 0)),
                 pl.BlockSpec((n_probe - 1, yc, nz, part), lambda y: (0, y, 0, 0)),
             ],
@@ -173,18 +180,11 @@
             compiler_params=params(),
             cost_estimate=cost(block * 2, block * 10),
             name="combine",
-        )(me, pre, back[v], *carried)
-        got = [
-            lax.ppermute(send[s - 1], "probe", [(p, (p + s) % n_probe) for p in range(n_probe)])
-            for s in range(1, n_probe)
-        ]
-        owns.append(own)
-        gots.append(got[0][None] if n_probe == 2 else jnp.stack(got))
-
-    sketch = None
-    for v in range(nvars):
+        )(me, pre, back, *carried)
+
+    def sketch_columns(v, own, got, sketch):
         carried = [] if sketch is None else [sketch]
-        sketch = pl.pallas_call(
+        return pl.pallas_call(
             sketch_kernel,
             grid=(ny // yc,),
             in_specs=[
@@ -192,13 +192,29 @@
                 pl.BlockSpec((yc, nz, part), lambda y: (y, 0, 0)),
                 pl.BlockSpec((n_probe - 1, yc, nz, part), lambda y: (0, y, 0, 0)),
             ] + [any_spec] * len(carried),
-            out_specs=pl.BlockSpec((columns, 1, yc, nz, part), lambda y, v=v: (0, v, y, 0, 0)),
+            out_specs=pl.BlockSpec((columns, 1, yc, nz, part), lambda y: (0, v, y, 0, 0)),
             out_shape=jax.ShapeDtypeStruct((columns, nvars, ny, nz, part), BF16),
             input_output_aliases={3: 0} if carried else {},
             compiler_params=params(),
             cost_estimate=cost(block * 4, block * 4),
             name="sketch_columns",
-        )(mix, owns[v], gots[v], *carried)
+        )(mix, own, got, *carried)
+
+    pres, sends, section, sketch = [], [], None, None
+    for v in range(nvars):
+        after = lines_z[1 : nvars - 1] if v == 0 else [pres[v - 1]]
+        if v == 1:
+            after.append(lines_z[-1])
+        if v >= 2:
+            after.append(sends[v - 2])
+        term = z_terms(v, after)
+        back = exchange(term).reshape(n_col * yb, nz, nx)[:ny]
+        pres.append(xy_terms(v, [term]))
+        section, own, send = combine(v, pres[v], back, section)
+        sends.append(send)
+        got = [passed(send[s - 1], s) for s in range(1, n_probe)]
+        got = got[0][None] if n_probe == 2 else jnp.stack(got)
+        sketch = sketch_columns(v, own, got, sketch)
     return (section[None], sketch)
 
 

time: 709 us -> 598 us (0.84)
  waiting for transfers between devices: 258 us -> 130 us
  blocking collectives: 222 us -> 176 us
  Pallas kernels: 167 us -> 198 us
  starting transfers between devices: 32.3 us -> 49.6 us
  local copies, waits for them, and re-layouts: 7.42 us -> 19.3 us
    all_to_all x6 -> x7, waiting for transfers between devices: 173 us -> 50.1 us  [exchange(): return lax.all_to_all(block, 'col', split_axis=0, concat_axis=0)]
    all_to_all x5 -> x4, blocking collectives: 222 us -> 176 us  [exchange(): return lax.all_to_all(block, 'col', split_axis=0, concat_axis=0)]
    pallas_call x16 -> x20, Pallas kernels: 167 us -> 198 us  [the longest x5 125 us: xy_terms(): pl.pallas_call(xy_kernel, grid=(nz // zb,), in_specs=[SMEM, one, one, adv...]
    all_to_all x6 -> x7, starting transfers between devices: 26.7 us -> 42.4 us  [exchange(): return lax.all_to_all(block, 'col', split_axis=0, concat_axis=0)]
    ppermute x5 -> x6, waiting for transfers between devices: 83.5 us -> 79.4 us  [passed(): lax.ppermute(block, 'probe', [(p, (p + shift) % n_probe) for p in range(n...]
  transfers between devices with their start and end apart: 12 -> 14, of which waited for: 10 -> 12; matrix products, arithmetic and copies ran while one was open for 2% -> 3% of each run, Pallas kernels for 23% -> 33%
where the time goes in v2:
time: 598 us; the launch traced here: 593 us
  Pallas kernels  198 us (33%)
  blocking collectives  176 us (29%)
  waiting for transfers between devices  130 us (22%)
  starting transfers between devices  49.6 us (8%)
  local copies, waits for them, and re-layouts  19.3 us (3%)
  between operations  14.4 us (2%)
    all_to_all x4, blocking collectives, exchange(): return lax.all_to_all(block, 'col', split_axis=0, concat_axis=0)  176 us
    pallas_call x5, Pallas kernels, xy_terms(): pl.pallas_call(xy_kernel, grid=(nz // zb,), in_specs=[SMEM, one, one, adv...  125 us
    ppermute x6, waiting for transfers between devices, passed(): lax.ppermute(block, 'probe', [(p, (p + shift) % n_probe) for p in range(n...  79.4 us
    all_to_all x7, waiting for transfers between devices, exchange(): return lax.all_to_all(block, 'col', split_axis=0, concat_axis=0)  50.1 us
    all_to_all x7, starting transfers between devices, exchange(): return lax.all_to_all(block, 'col', split_axis=0, concat_axis=0)  42.4 us
    pallas_call x5, Pallas kernels, z_terms(): pl.pallas_call(z_kernel, grid=(yb // ys,), in_specs=[SMEM, z_spec, z_spec...  26.3 us
    pallas_call x5, Pallas kernels, combine(): pl.pallas_call(combine_kernel, grid=(ny // yc,), in_specs=[SMEM, whole, w...  24.9 us
    pallas_call x5, Pallas kernels, sketch_columns(): pl.pallas_call(sketch_kernel, grid=(ny // yc,), in_specs=[SMEM, pl.BlockS...  21.8 us
  transfers between devices with their start and end apart: 14, of which 12 were waited for; matrix products, arithmetic and copies ran while one was open for 3% of the time, Pallas kernels for 33%

profile of v2, /device:TPU:0, one launch (start us, length us, event | category | flops | bytes accessed | tf_op | source)
XLA Modules:
  0.0 593.3 jit_solution(12098724855674886840)
XLA Ops:
  9.7 6.3 %all-to-all-start.1 = ((bf16[4,6,48,384]{3,2,1,0:T(8,128)(2,1)}), bf16[4,6,48,384]{3,2,1,0:T(8,128)(2,1)}, u32[]{:S(2)}, u32[]{:S(2)}) async-start(bf16[4,6,48,384]{3,2,1,0:T(8,128)(2,1)} %constant_dynamic-slice_fusion.2), calls=%async_computation.1 | async-start | bytes 1769472 | tf_op jit(solution)/shard_map/all_to_all | solution.py:91
  16.0 7.5 %fusion.15 = (bf16[1,1,48,48,384]{4,3,2,1,0:T(8,128)(2,1)}, bf16[1,1,48,48,384]{4,3,2,1,0:T(8,128)(2,1)}, bf16[1,1,48,48,384]{4,3,2,1,0:T(8,128)(2,1)S(1)}, bf16...) fusion(bf16[1,5,48,48,384]{4,3,2,1,0:T(8,128)(2,1)} %param.10), kind=kLoop, calls=%fused_computation.33 | loop fusion | bytes 17694720 | tf_op jit(solution)/shard_map/slice | solution.py:107
  23.5 14.8 %all-to-all-done.1 = bf16[4,6,48,384]{3,2,1,0:T(8,128)(2,1)} async-done(((bf16[4,6,48,384]{3,2,1,0:T(8,128)(2,1)}), bf16[4,6,48,384]{3,2,1,0:T(8,128)(2,1)}, u32[]{:S(2)}, u32[]{:S(2)}) %all-to-all-start.1) | async-done | bytes 884768 | tf_op jit(solution)/shard_map/all_to_all | solution.py:91
  38.3 45.3 %all_to_all.55.refs_1_.lines = bf16[4,12,48,384]{3,2,1,0:T(8,128)(2,1)} all-to-all(bf16[4,12,48,384]{3,2,1,0:T(8,128)(2,1)} %bitcast.58), channel_id=1, replica_groups=mesh['probe'=2,'row'=4,'col'=4] {'col'}, dimensions={0} | all-to-all | bytes 3538944 | tf_op jit(solution)/shard_map/all_to_all | solution.py:91
  83.6 43.6 %all_to_all.56.lines = bf16[4,12,48,384]{3,2,1,0:T(8,128)(2,1)} all-to-all(bf16[4,12,48,384]{3,2,1,0:T(8,128)(2,1)S(1)} %bitcast.57), channel_id=1, replica_groups=mesh['probe'=2,'row'=4,'col'=4] {'col'}, dimensions={0} | all-to-all | bytes 3538944 | tf_op jit(solution)/shard_map/all_to_all | solution.py:91
  127.2 43.6 %all_to_all.57.refs_2_.lines = bf16[4,12,48,384]{3,2,1,0:T(8,128)(2,1)} all-to-all(bf16[4,12,48,384]{3,2,1,0:T(8,128)(2,1)S(1)} %bitcast.56), channel_id=1, replica_groups=mesh['probe'=2,'row'=4,'col'=4] {'col'}, dimensions={0} | all-to-all | bytes 3538944 | tf_op jit(solution)/shard_map/all_to_all | solution.py:91
  170.8 43.6 %all_to_all.58.refs_0_.lines = bf16[4,12,48,384]{3,2,1,0:T(8,128)(2,1)} all-to-all(bf16[4,12,48,384]{3,2,1,0:T(8,128)(2,1)S(1)} %bitcast.55), channel_id=1, replica_groups=mesh['probe'=2,'row'=4,'col'=4] {'col'}, dimensions={0} | all-to-all | bytes 3538944 | tf_op jit(solution)/shard_map/all_to_all | solution.py:91
  222.7 16.9 %collective-permute-done = bf16[4,6,48,384]{3,2,1,0:T(8,128)(2,1)S(1)} collective-permute-done((bf16[4,6,48,384]{3,2,1,0:T(8,128)(2,1)}, bf16[4,6,48,384]{3,2,1,0:T(8,128)(2,1)S(1)}, u32[]{:S(2)}, u32[]{:S(2)}) %collective-permute-start) | collective-permute-done | bytes 884768 | tf_op jit(solution)/shard_map/ppermute | solution.py:99
  246.2 13.2 %all-to-all-done.refs_1_.lines = bf16[4,12,48,384]{3,2,1,0:T(8,128)(2,1)} async-done(((bf16[4,12,48,384]{3,2,1,0:T(8,128)(2,1)}), bf16[4,12,48,384]{3,2,1,0:T(8,128)(2,1)}, u32[]{:S(2)}, u32[]{:S(2)}) %all-to-all-start) | async-done | bytes 1769504 | tf_op jit(solution)/shard_map/all_to_all | solution.py:91
  264.2 5.9 %compare_select_fusion.mat_y = bf16[1536,3072]{1,0:T(8,128)(2,1)} fusion(s32[3072]{0:T(1024)S(1)} %get-tuple-element.45, s32[1536]{0:T(1024)S(1)} %get-tuple-element.47, bf16[96,192]{1,0:T(8,128)(2,1)S(1)} %bitcast.61, s32[3072]{0:T(1024)S(1)} %get-tuple-element.44, s32[1536]{0:T(1024)S(1)} %get-tuple-element.46), kind=kOutput, calls=%fused_computation | convolution fusion | flops 1878736896 | bytes 9510912 | tf_op jit(solution)/shard_map/dot_general | solution.py:117
  270.1 24.9 %xy_terms.5.refs_0_.pre = f32[48,48,384]{2,1,0:T(8,128)} custom-call(f32[1]{0:T(128)} %get-tuple-element.39.coef, bf16[5,48,48,384]{3,2,1,0:T(8,128)(2,1)} %bitcast.44, bf16[5,48,48,384]{3,2,1,0:T(8,128)(2,1)} %bitcast.49, bf16[48,48,384]{2,1,0:T(8,128)(2,1)} %adv_x.9, bf16[48,48,384]{2,1,0:T(8,128)(2,1)} %adv_y.9, ...), custom_call_target="tpu_custom_call" | custom-call | flops 12230590464 | bytes 14155776 | tf_op jit(solution)/shard_map/xy_terms/pallas_call | solution.py:146
  313.3 24.9 %xy_terms.6.refs_0_.pre = f32[48,48,384]{2,1,0:T(8,128)} custom-call(f32[1]{0:T(128)} %get-tuple-element.43.coef, bf16[5,48,48,384]{3,2,1,0:T(8,128)(2,1)} %bitcast.45, bf16[5,48,48,384]{3,2,1,0:T(8,128)(2,1)} %bitcast.50, bf16[48,48,384]{2,1,0:T(8,128)(2,1)} %adv_x.9, bf16[48,48,384]{2,1,0:T(8,128)(2,1)} %adv_y.9, ...), custom_call_target="tpu_custom_call" | custom-call | flops 12230590464 | bytes 14155776 | tf_op jit(solution)/shard_map/xy_terms/pallas_call | solution.py:146
  338.3 5.3 z_terms.7.refs_0_
  343.6 5.5 all-to-all-done.7
  353.4 24.9 %xy_terms.7.refs_0_.pre = f32[48,48,384]{2,1,0:T(8,128)} custom-call(f32[1]{0:T(128)} %get-tuple-element.40.coef, bf16[5,48,48,384]{3,2,1,0:T(8,128)(2,1)} %bitcast.46, bf16[5,48,48,384]{3,2,1,0:T(8,128)(2,1)} %bitcast.51, bf16[48,48,384]{2,1,0:T(8,128)(2,1)} %adv_x.9, bf16[48,48,384]{2,1,0:T(8,128)(2,1)} %adv_y.9, ...), custom_call_target="tpu_custom_call" | custom-call | flops 12230590464 | bytes 14155776 | tf_op jit(solution)/shard_map/xy_terms/pallas_call | solution.py:146
  385.7 5.3 z_terms.8.refs_0_
  394.2 14.5 %all-to-all-start.10 = ((bf16[4,12,48,384]{3,2,1,0:T(8,128)(2,1)}), bf16[4,12,48,384]{3,2,1,0:T(8,128)(2,1)}, u32[]{:S(2)}, u32[]{:S(2)}) async-start(bf16[4,12,48,384]{3,2,1,0:T(8,128)(2,1)} %z_terms.8.refs_0_), calls=%async_computation.10 | async-start | bytes 3538944 | tf_op jit(solution)/shard_map/all_to_all | solution.py:91
  414.7 25.0 %xy_terms.8.refs_0_.pre = f32[48,48,384]{2,1,0:T(8,128)} custom-call(f32[1]{0:T(128)} %get-tuple-element.41.coef, bf16[5,48,48,384]{3,2,1,0:T(8,128)(2,1)} %bitcast.47, bf16[5,48,48,384]{3,2,1,0:T(8,128)(2,1)} %bitcast.52, bf16[48,48,384]{2,1,0:T(8,128)(2,1)} %adv_x.9, bf16[48,48,384]{2,1,0:T(8,128)(2,1)} %adv_y.9, ...), custom_call_target="tpu_custom_call" | custom-call | flops 12230590464 | bytes 14155776 | tf_op jit(solution)/shard_map/xy_terms/pallas_call | solution.py:146
  439.8 5.3 z_terms.9.refs_0_
  463.7 24.9 %xy_terms.9.pre = f32[48,48,384]{2,1,0:T(8,128)} custom-call(f32[1]{0:T(128)} %get-tuple-element.42.coef, bf16[5,48,48,384]{3,2,1,0:T(8,128)(2,1)} %bitcast.48, bf16[5,48,48,384]{3,2,1,0:T(8,128)(2,1)} %bitcast.53, bf16[48,48,384]{2,1,0:T(8,128)(2,1)} %adv_x.9, bf16[48,48,384]{2,1,0:T(8,128)(2,1)} %adv_y.9, ...), custom_call_target="tpu_custom_call" | custom-call | flops 12230590464 | bytes 14155776 | tf_op jit(solution)/shard_map/xy_terms/pallas_call | solution.py:146
  488.6 5.8 all-to-all-done.9
  512.3 20.9 %collective-permute-done.3 = bf16[48,48,192]{2,1,0:T(8,128)(2,1)} collective-permute-done((bf16[48,48,192]{2,1,0:T(8,128)(2,1)}, bf16[48,48,192]{2,1,0:T(8,128)(2,1)}, u32[]{:S(2)}, u32[]{:S(2)}) %collective-permute-start.3) | collective-permute-done | bytes 884768 | tf_op jit(solution)/shard_map/ppermute | solution.py:99
  537.6 20.9 %collective-permute-done.2 = bf16[48,48,192]{2,1,0:T(8,128)(2,1)} collective-permute-done((bf16[48,48,192]{2,1,0:T(8,128)(2,1)}, bf16[48,48,192]{2,1,0:T(8,128)(2,1)}, u32[]{:S(2)}, u32[]{:S(2)}) %collective-permute-start.2) | collective-permute-done | bytes 884768 | tf_op jit(solution)/shard_map/ppermute | solution.py:99
  562.9 18.9 %collective-permute-done.1 = bf16[48,48,192]{2,1,0:T(8,128)(2,1)} collective-permute-done((bf16[48,48,192]{2,1,0:T(8,128)(2,1)}, bf16[48,48,192]{2,1,0:T(8,128)(2,1)}, u32[]{:S(2)}, u32[]{:S(2)}) %collective-permute-start.1) | collective-permute-done | bytes 884768 | tf_op jit(solution)/shard_map/ppermute | solution.py:99
  (82 shorter events, 111.0 us)
Async XLA Ops:
  7.2 262.9 %all-gather.2.cloned.1.call-start = ((), (), s32[]{:S(2)}) async-start(), calls=%async_computation.11 | async-start | bytes 44236800 | tf_op jit(solution)/shard_map/all_gather | solution.py:108
  9.7 28.6 %all-to-all-start.1 = ((bf16[4,6,48,384]{3,2,1,0:T(8,128)(2,1)}), bf16[4,6,48,384]{3,2,1,0:T(8,128)(2,1)}, u32[]{:S(2)}, u32[]{:S(2)}) async-start(bf16[4,6,48,384]{3,2,1,0:T(8,128)(2,1)} %constant_dynamic-slice_fusion.2), calls=%async_computation.1 | async-start | bytes 1769472 | tf_op jit(solution)/shard_map/all_to_all | solution.py:91
  38.3 45.3 %copy-start.15 = (bf16[1,1,48,48,384]{4,3,2,1,0:T(8,128)(2,1)S(1)}, bf16[1,1,48,48,384]{4,3,2,1,0:T(8,128)(2,1)}, u32[]{:S(2)}) copy-start(bf16[1,1,48,48,384]{4,3,2,1,0:T(8,128)(2,1)} %get-tuple-element.32) | copy-start | bytes 5308420
  214.4 6.1 %copy-start.18 = (f32[5]{0:T(128)S(1)}, f32[5]{0:T(128)}, u32[]{:S(2)}) copy-start(f32[5]{0:T(128)} %param.15) | copy-start | bytes 64
  214.4 45.0 %all-to-all-start = ((bf16[4,12,48,384]{3,2,1,0:T(8,128)(2,1)}), bf16[4,12,48,384]{3,2,1,0:T(8,128)(2,1)}, u32[]{:S(2)}, u32[]{:S(2)}) async-start(bf16[4,12,48,384]{3,2,1,0:T(8,128)(2,1)} %bitcast.6), calls=%async_computation | async-start | bytes 3538944 | tf_op jit(solution)/shard_map/all_to_all | solution.py:91
  219.0 20.6 %collective-permute-start = (bf16[4,6,48,384]{3,2,1,0:T(8,128)(2,1)}, bf16[4,6,48,384]{3,2,1,0:T(8,128)(2,1)S(1)}, u32[]{:S(2)}, u32[]{:S(2)}) collective-permute-start(bf16[4,6,48,384]{3,2,1,0:T(8,128)(2,1)} %all-to-all-done.1), channel_id=1, source_target_pairs={{0,16},{16,0},{1,17},{17,1},{2,18},{18,2},{3,19},{19,3},{4,20},{20... | collective-permute-start | bytes 2654216 | tf_op jit(solution)/shard_map/ppermute | solution.py:99
  221.3 19.7 %copy-start.2 = (bf16[2,192,192]{2,1,0:T(8,128)(2,1)S(1)}, bf16[2,192,192]{2,1,0:T(8,128)(2,1)}, u32[]{:S(2)}) copy-start(bf16[2,192,192]{2,1,0:T(8,128)(2,1)} %param.18) | copy-start | bytes 442372
  246.2 16.8 %copy-start.17 = (bf16[2,384,384]{2,1,0:T(8,128)(2,1)S(1)}, bf16[2,384,384]{2,1,0:T(8,128)(2,1)}, u32[]{:S(2)}) copy-start(bf16[2,384,384]{2,1,0:T(8,128)(2,1)} %param.16) | copy-start | bytes 1769476
  259.5 44.2 %all-to-all-start.6 = ((bf16[4,12,48,384]{3,2,1,0:T(8,128)(2,1)}), bf16[4,12,48,384]{3,2,1,0:T(8,128)(2,1)S(1)}, u32[]{:S(2)}, u32[]{:S(2)}) async-start(bf16[4,12,48,384]{3,2,1,0:T(8,128)(2,1)} %z_terms.5.refs_0_), calls=%async_computation.6 | async-start | bytes 3538944 | tf_op jit(solution)/shard_map/all_to_all | solution.py:91
  303.7 45.4 %all-to-all-start.7 = ((bf16[4,12,48,384]{3,2,1,0:T(8,128)(2,1)}), bf16[4,12,48,384]{3,2,1,0:T(8,128)(2,1)}, u32[]{:S(2)}, u32[]{:S(2)}) async-start(bf16[4,12,48,384]{3,2,1,0:T(8,128)(2,1)} %z_terms.6.refs_0_), calls=%async_computation.7 | async-start | bytes 3538944 | tf_op jit(solution)/shard_map/all_to_all | solution.py:91
  313.3 24.9 %copy-start.3 = (bf16[1,48,48,192]{3,2,1,0:T(8,128)(2,1)S(1)}, bf16[1,48,48,192]{3,2,1,0:T(8,128)(2,1)}, u32[]{:S(2)}) copy-start(bf16[1,48,48,192]{3,2,1,0:T(8,128)(2,1)} %get-tuple-element.17.refs_1_) | copy-start | bytes 2654212
  349.1 45.1 %all-to-all-start.8 = ((bf16[4,12,48,384]{3,2,1,0:T(8,128)(2,1)}), bf16[4,12,48,384]{3,2,1,0:T(8,128)(2,1)}, u32[]{:S(2)}, u32[]{:S(2)}) async-start(bf16[4,12,48,384]{3,2,1,0:T(8,128)(2,1)} %z_terms.7.refs_0_), calls=%async_computation.8 | async-start | bytes 3538944 | tf_op jit(solution)/shard_map/all_to_all | solution.py:91
  394.2 55.0 %all-to-all-start.10 = ((bf16[4,12,48,384]{3,2,1,0:T(8,128)(2,1)}), bf16[4,12,48,384]{3,2,1,0:T(8,128)(2,1)}, u32[]{:S(2)}, u32[]{:S(2)}) async-start(bf16[4,12,48,384]{3,2,1,0:T(8,128)(2,1)} %z_terms.8.refs_0_), calls=%async_computation.10 | async-start | bytes 3538944 | tf_op jit(solution)/shard_map/all_to_all | solution.py:91
  414.7 25.1 %copy-start.9 = (bf16[1,48,48,192]{3,2,1,0:T(8,128)(2,1)S(1)}, bf16[1,48,48,192]{3,2,1,0:T(8,128)(2,1)}, u32[]{:S(2)}) copy-start(bf16[1,48,48,192]{3,2,1,0:T(8,128)(2,1)} %get-tuple-element.21.refs_1_) | copy-start | bytes 2654212
  449.2 45.2 %all-to-all-start.9 = ((bf16[4,12,48,384]{3,2,1,0:T(8,128)(2,1)}), bf16[4,12,48,384]{3,2,1,0:T(8,128)(2,1)}, u32[]{:S(2)}, u32[]{:S(2)}) async-start(bf16[4,12,48,384]{3,2,1,0:T(8,128)(2,1)} %z_terms.9.refs_0_), calls=%async_computation.9 | async-start | bytes 3538944 | tf_op jit(solution)/shard_map/all_to_all | solution.py:91
  453.6 48.3 %collective-permute-start.5 = (bf16[48,48,192]{2,1,0:T(8,128)(2,1)S(1)}, bf16[48,48,192]{2,1,0:T(8,128)(2,1)}, u32[]{:S(2)}, u32[]{:S(2)}) collective-permute-start(bf16[48,48,192]{2,1,0:T(8,128)(2,1)S(1)} %bitcast.41), channel_id=1, source_target_pairs={{0,16},{16,0},{1,17},{17,1},{2,18},{18,2},{3,19},{19,3},{4,20},{20... | collective-permute-start | bytes 2654216 | tf_op jit(solution)/shard_map/ppermute | solution.py:99
  455.2 52.8 %collective-permute-start.4 = (bf16[48,48,192]{2,1,0:T(8,128)(2,1)}, bf16[48,48,192]{2,1,0:T(8,128)(2,1)}, u32[]{:S(2)}, u32[]{:S(2)}) collective-permute-start(bf16[48,48,192]{2,1,0:T(8,128)(2,1)} %bitcast.42), channel_id=1, source_target_pairs={{0,16},{16,0},{1,17},{17,1},{2,18},{18,2},{3,19},{19,3},{4,20},{20... | collective-permute-start | bytes 2654216 | tf_op jit(solution)/shard_map/ppermute | solution.py:99
  455.7 77.5 %collective-permute-start.3 = (bf16[48,48,192]{2,1,0:T(8,128)(2,1)}, bf16[48,48,192]{2,1,0:T(8,128)(2,1)}, u32[]{:S(2)}, u32[]{:S(2)}) collective-permute-start(bf16[48,48,192]{2,1,0:T(8,128)(2,1)} %bitcast.43), channel_id=1, source_target_pairs={{0,16},{16,0},{1,17},{17,1},{2,18},{18,2},{3,19},{19,3},{4,20},{20... | collective-permute-start | bytes 2654216 | tf_op jit(solution)/shard_map/ppermute | solution.py:99
  463.2 95.4 %collective-permute-start.2 = (bf16[48,48,192]{2,1,0:T(8,128)(2,1)}, bf16[48,48,192]{2,1,0:T(8,128)(2,1)}, u32[]{:S(2)}, u32[]{:S(2)}) collective-permute-start(bf16[48,48,192]{2,1,0:T(8,128)(2,1)} %bitcast.62), channel_id=1, source_target_pairs={{0,16},{16,0},{1,17},{17,1},{2,18},{18,2},{3,19},{19,3},{4,20},{20... | collective-permute-start | bytes 2654216 | tf_op jit(solution)/shard_map/ppermute | solution.py:99
  494.4 7.5 %copy-start.19 = (f32[2,2]{1,0:T(2,128)S(1)}, f32[2,2]{1,0:T(2,128)}, u32[]{:S(2)}) copy-start(f32[2,2]{1,0:T(2,128)} %param.19) | copy-start | bytes 52
  500.4 81.5 %collective-permute-start.1 = (bf16[48,48,192]{2,1,0:T(8,128)(2,1)}, bf16[48,48,192]{2,1,0:T(8,128)(2,1)}, u32[]{:S(2)}, u32[]{:S(2)}) collective-permute-start(bf16[48,48,192]{2,1,0:T(8,128)(2,1)} %bitcast.63), channel_id=1, source_target_pairs={{0,16},{16,0},{1,17},{17,1},{2,18},{18,2},{3,19},{19,3},{4,20},{20... | collective-permute-start | bytes 2654216 | tf_op jit(solution)/shard_map/ppermute | solution.py:99
  508.0 25.3 %copy-start.8 = (bf16[48,48,192]{2,1,0:T(8,128)(2,1)S(1)}, bf16[48,48,192]{2,1,0:T(8,128)(2,1)}, u32[]{:S(2)}) copy-start(bf16[48,48,192]{2,1,0:T(8,128)(2,1)} %copy-done.7) | copy-start | bytes 2654212
  533.3 25.3 %copy-start.11 = (bf16[48,48,192]{2,1,0:T(8,128)(2,1)S(1)}, bf16[48,48,192]{2,1,0:T(8,128)(2,1)}, u32[]{:S(2)}) copy-start(bf16[48,48,192]{2,1,0:T(8,128)(2,1)} %copy-done.10) | copy-start | bytes 2654212
  558.6 23.3 %copy-start.13 = (bf16[48,48,192]{2,1,0:T(8,128)(2,1)S(1)}, bf16[48,48,192]{2,1,0:T(8,128)(2,1)}, u32[]{:S(2)}) copy-start(bf16[48,48,192]{2,1,0:T(8,128)(2,1)} %copy-done.12) | copy-start | bytes 2654212
  (10 other events, 23.2 us)
Sparse Core Ops, SparseCore 0:
  9.6 216.8 all-gather.1
